TPU v7x, 128 devices: a whole 4x4x4 slice. The times are simulated.
128 devices in a mesh: section: 16 (over z, y_lo, core), tensor: 8 (over y_hi, x).
Axes of the slice: x: 4, y: 4 (y_hi: 2, y_lo: 2; y = y_hi * 2 + y_lo), z: 4, core: 2. Of those that a mesh axis runs over, the one named last changes fastest.
Arguments:
- token_ids: int32 [4096], P('section'), may hold values from 0 to 152063, as said below
- column_order: int32 [8192], replicated, may hold values from 0 to 8191, each once
- residual: bfloat16 [4096, 8192], P('section', 'tensor'), may hold values from -40 to 40
- attn_out: bfloat16 [4096, 8192], P('section', 'tensor'), may hold values from -6 to 6
- out_proj: bfloat16 [8192, 8192], P(None, 'tensor'), may hold values from -0.0625 to 0.0625
- norm_gain: float32 [8192], P('tensor'), may hold values from 0.5 to 1.5
Outputs:
- factored: float32 [8192, 8192], P('section', 'tensor')
Inputs may be any that keep to these rules, and one draw needn't show every extreme that they name: `token_ids`: id 0 marks padding. In each block of 256 tokens of one section index the padding fills trailing positions, and each block holds at least one non-padding token.
All inputs are finite; a program needn't handle non-finite values.
Results may differ from a plain program's by a relative error of at most 0.0067.
Values may be sent and summed in bfloat16 or wider, within the bound.
No kernel may reach another device: no remote copies, remote signals or barrier semaphores. Data moves between devices by JAX's collectives and lax.ppermute only.
A program may use at most 128 MiB of HBM per device.

v0:
```python
import jax
import jax.numpy as jnp
from jax import lax
from jax.sharding import PartitionSpec as P

TILE = 128
PANEL = 1024
epsilon = 1e-06


def spread(value, axis, source):
    kept = jnp.where(lax.axis_index(axis) == source, value, 0).astype(value.dtype)
    return lax.psum(kept, axis)


def shards(token_ids, column_order, residual, attn_out, out_proj, norm_gain):
    section_count = lax.axis_size("section")
    tensor_count = lax.axis_size("tensor")
    section_id = lax.axis_index("section")
    tensor_id = lax.axis_index("tensor")
    model_width = out_proj.shape[0]
    span_rows = model_width // section_count
    span_cols = model_width // tensor_count
    projected = jnp.dot(
        lax.all_gather(attn_out, "tensor", axis=1, tiled=True),
        out_proj,
        preferred_element_type=jnp.float32,
    )
    rounded = (residual.astype(jnp.float32) + projected).astype(jnp.bfloat16)
    hidden = lax.optimization_barrier(rounded).astype(jnp.float32)
    squares = lax.psum(jnp.sum(hidden * hidden, axis=1), "tensor")
    kept_rows = (token_ids != 0).astype(jnp.float32)
    token_count = lax.psum(jnp.sum(kept_rows), "section")
    row_scale = lax.rsqrt(squares / model_width + epsilon) * kept_rows
    normed = (hidden * row_scale[:, None] * norm_gain[None, :]).astype(jnp.bfloat16)
    target = jnp.arange(section_count, dtype=jnp.int32)[:, None, None]
    tile_index = jnp.arange(span_rows // TILE, dtype=jnp.int32)[None, :, None]
    offset = jnp.arange(TILE, dtype=jnp.int32)[None, None, :]
    send_global = ((tile_index * section_count + target) * TILE + offset).reshape(model_width)
    col_tiles = jnp.arange(span_cols // TILE, dtype=jnp.int32)[:, None]
    cols_global = (
        (col_tiles * tensor_count + tensor_id) * TILE + jnp.arange(TILE, dtype=jnp.int32)[None, :]
    ).reshape(span_cols)
    full_rows = lax.all_gather(normed, "tensor", axis=1, tiled=True)
    outgoing = jnp.take(full_rows, jnp.take(column_order, send_global), axis=1)
    mine_rows = lax.all_to_all(outgoing, "section", split_axis=1, concat_axis=0, tiled=True)
    col_part = jnp.take(full_rows, jnp.take(column_order, cols_global), axis=1)
    gram_sum = lax.dot_general(
        mine_rows,
        lax.all_gather(col_part, "section", axis=0, tiled=True),
        (((0,), (0,)), ((), ())),
        preferred_element_type=jnp.float32,
    )
    hessian = gram_sum / token_count
    panel_local = PANEL // tensor_count
    per_group = panel_local // TILE
    gathered = lax.all_gather(hessian[:, :panel_local], "tensor", axis=1, tiled=True)
    panel_rows = (
        gathered.reshape(span_rows, tensor_count, per_group, TILE)
        .transpose(0, 2, 1, 3)
        .reshape(span_rows, PANEL)
    )
    first_tile = panel_rows[:TILE]
    stacked = lax.all_gather(first_tile, "section", axis=0, tiled=True)
    diag_block = stacked[:PANEL]
    chol_low = jnp.linalg.cholesky(diag_block)
    own_lower = lax.linalg.triangular_solve(
        chol_low, panel_rows, left_side=False, lower=True, transpose_a=True
    )
    copies = [
        spread(own_lower, "section", tensor_id + second * tensor_count)
        for second in range(section_count // tensor_count)
    ]
    shaped = [copy_rows.reshape(span_rows // TILE, TILE, PANEL) for copy_rows in copies]
    other_lower = jnp.stack(shaped, axis=1).reshape(span_cols, PANEL)
    row_tiles = jnp.arange(span_rows // TILE, dtype=jnp.int32)[:, None]
    rows_global = (
        (row_tiles * section_count + section_id) * TILE + jnp.arange(TILE, dtype=jnp.int32)[None, :]
    ).reshape(span_rows)
    panel_global = cols_global[:panel_local]
    left_part = jnp.take(own_lower, panel_global, axis=1)
    left_part = jnp.where(
        rows_global[:, None] >= panel_global[None, :], left_part, jnp.float32(0.0)
    )
    update = jnp.dot(
        own_lower,
        other_lower[panel_local:].T,
        precision=lax.Precision.HIGHEST,
        preferred_element_type=jnp.float32,
    )
    right_part = hessian[:, panel_local:] - update
    return jnp.concatenate([left_part, right_part], axis=1)


def solution(mesh):
    placed = (
        P("section"),
        P(),
        P("section", "tensor"),
        P("section", "tensor"),
        P(None, "tensor"),
        P("tensor"),
    )
    return jax.shard_map(
        shards, mesh=mesh, in_specs=placed, out_specs=P("section", "tensor"), check_vma=False
    )
```

profile of v0, /device:TPU:0, one launch (start us, length us, event | category | flops | bytes accessed | tf_op | source)
XLA Modules:
  0.0 999.8 jit_solution(9918803187925176559)
XLA Ops:
  7.3 76.3 %all-gather.6.cloned.1.call-done = bf16[256,8192]{1,0:T(8,128)(2,1)} async-done(((bf16[256,1024]{1,0:T(8,128)(2,1)}), bf16[256,8192]{1,0:T(8,128)(2,1)}) %all-gather.6.cloned.1.call-update) | async-done | bytes 4194320 | tf_op jit(solution)/shard_map/all_gather | solution.py:25
  83.7 11.5 %fusion.5 = bf16[256,1024]{1,0:T(8,128)(2,1)S(1)} fusion(bf16[256,8192]{1,0:T(8,128)(2,1)} %all-gather.6.cloned.1.call-done, bf16[8192,1024]{1,0:T(8,128)(2,1)} %param.10, bf16[256,1024]{1,0:T(8,128)(2,1)} %param.8), kind=kOutput, calls=%fused_computation.21 | convolution fusion | flops 4295753728 | bytes 22020096 | tf_op jit(solution)/shard_map/dot_general | solution.py:24
  95.3 19.8 %psum.28 = f32[256]{0:T(256)S(1)} all-reduce(f32[256]{0:T(256)S(1)} %fusion.6), channel_id=1, replica_groups=mesh['section'=16,'tensor'=8] {'tensor'}, use_global_device_ids=true, to_apply=%region_1.0 | all-reduce | flops 256 | bytes 2048 | tf_op jit(solution)/shard_map/psum | solution.py:31
  117.0 6.2 gather_fusion.2
  123.2 64.0 %all-gather.8.cloned.1.call-done = bf16[256,8192]{1,0:T(8,128)(2,1)} async-done(((bf16[256,1024]{1,0:T(8,128)(2,1)}), bf16[256,8192]{1,0:T(8,128)(2,1)}) %all-gather.8.cloned.1.call-update) | async-done | bytes 4194320 | tf_op jit(solution)/shard_map/all_gather | solution.py:44
  187.3 6.4 copy.13
  193.6 6.2 gather_fusion.3
  201.0 45.5 %gather_fusion = s32[8192]{0:T(1024)S(1)} fusion(s32[8192]{0:T(1024)S(1)} %copy-done, s32[8192]{0:T(1024)S(1)} %broadcast_clamp_fusion.1), kind=kCustom, calls=%fused_computation | custom fusion | bytes 98304 | tf_op jit(solution)/shard_map/jit(_take)/gather | solution.py:45
  246.7 33.9 %gather_fusion.1 = bf16[8192,256]{1,0:T(8,128)(2,1)} fusion(bf16[256,8192]{0,1:T(8,128)(2,1)} %copy.13, s32[8192]{0:T(1024)S(1)} %broadcast_clamp_fusion), kind=kCustom, calls=%fused_computation.1 | custom fusion | bytes 8421376 | tf_op jit(solution)/shard_map/jit(_take)/gather | solution.py:45
  280.6 6.4 copy.14
  287.0 4.6 broadcast_select_fusion
  291.6 4.6 all-to-all-start
  296.2 72.6 %psum.29 = f32[]{:T(128)} all-reduce(f32[]{:T(128)} %get-tuple-element.74), channel_id=1, replica_groups=mesh['section'=16,'tensor'=8] {'section'}, use_global_device_ids=true, to_apply=%region_3.0 | all-reduce | flops 1 | bytes 8 | tf_op jit(solution)/shard_map/psum | solution.py:33
  368.9 8.8 convolution_divide_fusion
  379.8 51.4 %all-gather.12.cloned.1.call-done = f32[512,1024]{0,1:T(8,128)} async-done(((f32[512,128]{0,1:T(8,128)}), f32[512,1024]{0,1:T(8,128)}) %all-gather.12.cloned.1.call-update) | async-done | bytes 2097168 | tf_op jit(solution)/shard_map/all_gather | solution.py:57
  433.3 59.7 %all-gather.14.cloned.1.call-done = f32[2048,1024]{0,1:T(8,128)} async-done(((f32[128,1024]{0,1:T(8,128)}), f32[2048,1024]{0,1:T(8,128)}) %all-gather.14.cloned.1.call-update) | async-done | bytes 8388624 | tf_op jit(solution)/shard_map/all_gather | solution.py:64
  493.0 4.7 slice.274
  497.8 5.5 copy.17
  503.2 4.4 fusion
  509.7 11.7 %cholesky.223 = f32[128,128]{1,0:T(8,128)S(1)} custom-call(f32[128,128]{1,0:T(8,128)S(1)} %cholesky.580), custom_call_target="Cholesky" | custom-call | tf_op jit(solution)/shard_map/jit(cholesky)/cholesky | solution.py:66
  521.5 9.8 custom-call.62
  531.3 2.6 cholesky.255
  533.8 2.4 constant_dynamic-update-slice_fusion.32
  537.8 11.9 %cholesky.244 = f32[128,128]{1,0:T(8,128)S(1)} custom-call(f32[128,128]{1,0:T(8,128)S(1)} %cholesky.584), custom_call_target="Cholesky" | custom-call | tf_op jit(solution)/shard_map/jit(cholesky)/cholesky | solution.py:66
  550.3 9.8 custom-call.63
  563.5 11.7 %cholesky.468 = f32[128,128]{1,0:T(8,128)S(1)} custom-call(f32[128,128]{1,0:T(8,128)S(1)} %cholesky.589), custom_call_target="Cholesky" | custom-call | tf_op jit(solution)/shard_map/jit(cholesky)/cholesky | solution.py:66
  576.5 9.8 custom-call.64
  587.5 2.3 convolution_subtract_fusion.2
  589.8 12.1 %cholesky.487 = f32[128,128]{1,0:T(8,128)S(1)} custom-call(f32[128,128]{1,0:T(8,128)S(1)} %cholesky.594), custom_call_target="Cholesky" | custom-call | tf_op jit(solution)/shard_map/jit(cholesky)/cholesky | solution.py:66
  603.2 9.8 custom-call.65
  614.1 2.3 convolution_subtract_fusion.10
  616.5 11.7 %cholesky.506 = f32[128,128]{1,0:T(8,128)S(1)} custom-call(f32[128,128]{1,0:T(8,128)S(1)} %cholesky.599), custom_call_target="Cholesky" | custom-call | tf_op jit(solution)/shard_map/jit(cholesky)/cholesky | solution.py:66
  629.5 9.9 custom-call.66
  640.5 2.3 convolution_subtract_fusion.11
  642.7 11.7 %cholesky.526 = f32[128,128]{1,0:T(8,128)S(1)} custom-call(f32[128,128]{1,0:T(8,128)S(1)} %cholesky.604), custom_call_target="Cholesky" | custom-call | tf_op jit(solution)/shard_map/jit(cholesky)/cholesky | solution.py:66
  655.8 9.8 custom-call.67
  668.6 11.9 %cholesky.546 = f32[128,128]{1,0:T(8,128)S(1)} custom-call(f32[128,128]{1,0:T(8,128)S(1)} %cholesky.609), custom_call_target="Cholesky" | custom-call | tf_op jit(solution)/shard_map/jit(cholesky)/cholesky | solution.py:66
  681.8 9.8 custom-call.68
  694.3 11.7 %cholesky.564 = f32[128,128]{1,0:T(8,128)S(1)} custom-call(f32[128,128]{1,0:T(8,128)S(1)} %convolution_subtract_fusion.13), custom_call_target="Cholesky" | custom-call | tf_op jit(solution)/shard_map/jit(cholesky)/cholesky | solution.py:66
  712.9 4.9 select_select_fusion
  717.8 22.9 %while.1 = (s32[]{:T(128)}, f32[1024,1024]{1,0:T(8,128)}, s32[8,2]{0,1:T(2,128)S(1)}, f32[8,128,128]{2,1,0:T(8,128)S(1)}, s32[]{:T(128)}) while((s32[]{:T(128)}, f32[1024,1024]{1,0:T(8,128)}, s32[8,2]{0,1:T(2,128)S(1)}, f32[8,128,128]{2,1,0:T(8,128)S(1)}, s32[]{:T(128)}) %tuple.59), condition=%wide.while_cond, body=%wide.while_body.sunk | while | flops 2 | bytes 131181 | solution.py:67
  740.7 79.0 %custom-call.69 = f32[8,128,128]{1,2,0:T(8,128)S(1)} custom-call(f32[8,128,128]{2,1,0:T(8,128)S(1)} %get-tuple-element.12), custom_call_target="InvertDiagBlocksLowerTriangular" | custom-call | tf_op jit(solution)/shard_map/triangular_solve | solution.py:67
  836.8 2.7 broadcast_select_fusion.2
  839.5 2.9 copy.24
  842.5 3.0 copy.25
  846.5 135.4 %all-reduce.4.cloned.1.call-done = (f32[4,1,128,1024]{3,2,1,0:T(8,128)}, f32[4,1,128,1024]{3,2,1,0:T(8,128)}) async-done(((f32[4,1,128,1024]{3,2,1,0:T(8,128)}, f32[4,1,128,1024]{3,2,1,0:T(8,128)}), (f32[4,1,128,1024]{3,2,1,0:T(8,128)}, f32[4,1,128,1024]{3,2,1,0:T(8,128)})) %all-reduce.4.cloned.1.call-update) | async-done | bytes 4194320 | tf_op jit(solution)/shard_map/psum | solution.py:13
  981.9 2.7 pad_maximum_fusion
  984.8 6.0 slice_subtract_fusion
  (136 shorter events, 76.3 us)
Async XLA Ops:
  6.5 110.4 %copy-start = (s32[8192]{0:T(1024)S(1)}, s32[8192]{0:T(1024)}, u32[]{:S(2)}) copy-start(s32[8192]{0:T(1024)} %param.7) | copy-start | bytes 98308
  6.5 77.1 %all-gather.6.cloned.1.call-start = ((), (), s32[]{:S(2)}) async-start(), calls=%async_computation.1 | async-start | bytes 4718592 | tf_op jit(solution)/shard_map/all_gather | solution.py:25
  7.3 107.8 %copy-start.7 = (s32[256]{0:T(256)S(1)}, s32[256]{0:T(256)}, u32[]{:S(2)}) copy-start(s32[256]{0:T(256)} %param.6) | copy-start | bytes 3076
  7.3 108.5 %copy-start.6 = (f32[1024]{0:T(1024)S(1)}, f32[1024]{0:T(1024)}, u32[]{:S(2)}) copy-start(f32[1024]{0:T(1024)} %param.11) | copy-start | bytes 12292
  7.3 180.0 %all-gather.8.cloned.1.call-start = ((), (), s32[]{:S(2)}) async-start(), calls=%async_computation.2 | async-start | bytes 4718592 | tf_op jit(solution)/shard_map/all_gather | solution.py:44
  116.8 252.1 %all-gather.10.cloned.1.call-start = ((), (), s32[]{:S(2)}) async-start(), calls=%async_computation.3 | async-start | bytes 8912896 | tf_op jit(solution)/shard_map/all_gather | solution.py:50
  291.6 77.3 %all-to-all-start = ((bf16[256,16,512]{2,0,1:T(8,128)(2,1)}), bf16[256,16,512]{2,0,1:T(8,128)(2,1)}, u32[]{:S(2)}, u32[]{:S(2)}) async-start(bf16[256,16,512]{2,0,1:T(8,128)(2,1)} %broadcast_select_fusion), calls=%async_computation | async-start | bytes 8388608 | tf_op jit(solution)/shard_map/all_to_all | solution.py:46
  296.2 135.1 %all-gather.12.cloned.1.call-start = ((), (), s32[]{:S(2)}) async-start(), calls=%async_computation.4 | async-start | bytes 2359296 | tf_op jit(solution)/shard_map/all_gather | solution.py:57
  377.7 1.3 copy-start.3
  379.8 113.2 %all-gather.14.cloned.1.call-start = ((), (), s32[]{:S(2)}) async-start(), calls=%async_computation.5 | async-start | bytes 8912896 | tf_op jit(solution)/shard_map/all_gather | solution.py:64
  433.2 548.8 %all-reduce.4.cloned.1.call-start = ((), (), s32[]{:S(2)}) async-start(), calls=%async_computation.6 | async-start | bytes 8388608 | tf_op jit(solution)/shard_map/psum | solution.py:13
  507.7 2.0 copy-start.2
  821.1 6.1 copy-start.5
  981.9 2.9 copy-start.4
  984.8 8.0 copy-start.1
Sparse Core Ops, SparseCore 0:
  9.7 73.9 all-gather.5
  116.9 70.3 all-gather.7
  201.0 58.7 all-gather.9
  379.9 51.3 all-gather.11
  433.3 59.6 all-gather.13
  845.7 136.2 all-reduce.3
where the time goes:
time: 1010 us; the launch traced here: 1000 us
  waiting for transfers between devices  388 us (38%)
  other arithmetic  274 us (27%)
  local copies, waits for them, and re-layouts  155 us (15%)
  blocking collectives  92.4 us (9%)
  matrix products  66.5 us (7%)
  between operations  19.2 us (2%)
    another operation x30, other arithmetic, shards(): chol_low = jnp.linalg.cholesky(diag_block)  172 us
    psum x1, waiting for transfers between devices, spread(): return lax.psum(kept, axis)  135 us
    gather x4, local copies, waits for them, and re-layouts, shards(): outgoing = jnp.take(full_rows, jnp.take(column_order, send_global), axis=1)  85.8 us
    another operation x3, other arithmetic, shards(): lax.linalg.triangular_solve(chol_low, panel_rows, left_side=False, lower=...  83.9 us
    all_gather x1, waiting for transfers between devices, shards(): lax.all_gather(attn_out, 'tensor', axis=1, tiled=True)  76.3 us
    psum x1, blocking collectives, shards(): token_count = lax.psum(jnp.sum(kept_rows), 'section')  72.6 us
    all_gather x1, waiting for transfers between devices, shards(): full_rows = lax.all_gather(normed, 'tensor', axis=1, tiled=True)  64 us
    all_gather x1, waiting for transfers between devices, shards(): stacked = lax.all_gather(first_tile, 'section', axis=0, tiled=True)  59.7 us
  transfers between devices with their start and end apart: 7, of which 5 were waited for; matrix products, arithmetic and copies ran while one was open for 10% of the time, Pallas kernels for 0%

commit v1 on v0

--- a/solution.py
+++ b/solution.py
@@ -10,7 +10,7 @@
 
 def spread(value, axis, source):
     kept = jnp.where(lax.axis_index(axis) == source, value, 0).astype(value.dtype)
-    return lax.psum(kept, axis)
+    return jnp.sum(lax.all_gather(kept, axis), axis=0)
 
 
 def shards(token_ids, column_order, residual, attn_out, out_proj, norm_gain):

time: 1010 us -> 1230 us (1.22)
  waiting for transfers between devices: 388 us -> 578 us
  other arithmetic: 274 us -> 301 us
    all_gather x0 -> x2, waiting for transfers between devices: none -> 326 us  [spread(): return jnp.sum(lax.all_gather(kept, axis), axis=0)]
    psum x1 -> x0, waiting for transfers between devices: 135 us -> none  [spread(): return lax.psum(kept, axis)]
    reduce_sum x0 -> x2, other arithmetic: none -> 26.8 us  [spread(): return jnp.sum(lax.all_gather(kept, axis), axis=0)]
    another operation x26 -> x24, local copies, waits for them, and re-layouts: 28.7 us -> 22.7 us
    another operation x30 -> x31, other arithmetic: 172 us -> 173 us  [shards(): chol_low = jnp.linalg.cholesky(diag_block)]
  transfers between devices with their start and end apart: 7 -> 8, of which waited for: 5 -> 6; matrix products, arithmetic and copies ran while one was open for 10% -> 9% of each run, Pallas kernels for 0% -> 0%
where the time goes in v1:
time: 1230 us; the launch traced here: 1220 us
  waiting for transfers between devices  578 us (47%)
  other arithmetic  301 us (24%)
  local copies, waits for them, and re-layouts  155 us (13%)
  blocking collectives  92.3 us (8%)
  matrix products  66.1 us (5%)
  between operations  19.3 us (2%)
    all_gather x2, waiting for transfers between devices, spread(): return jnp.sum(lax.all_gather(kept, axis), axis=0)  326 us
    another operation x31, other arithmetic, shards(): chol_low = jnp.linalg.cholesky(diag_block)  173 us
    gather x4, local copies, waits for them, and re-layouts, shards(): outgoing = jnp.take(full_rows, jnp.take(column_order, send_global), axis=1)  85.7 us
    another operation x3, other arithmetic, shards(): lax.linalg.triangular_solve(chol_low, panel_rows, left_side=False, lower=...  83.8 us
    all_gather x1, waiting for transfers between devices, shards(): lax.all_gather(attn_out, 'tensor', axis=1, tiled=True)  76.3 us
    psum x1, blocking collectives, shards(): token_count = lax.psum(jnp.sum(kept_rows), 'section')  72.6 us
    all_gather x1, waiting for transfers between devices, shards(): full_rows = lax.all_gather(normed, 'tensor', axis=1, tiled=True)  64 us
    all_gather x1, waiting for transfers between devices, shards(): stacked = lax.all_gather(first_tile, 'section', axis=0, tiled=True)  59.7 us
  transfers between devices with their start and end apart: 8, of which 6 were waited for; matrix products, arithmetic and copies ran while one was open for 9% of the time, Pallas kernels for 0%

profile of v1, /device:TPU:0, one launch (start us, length us, event | category | flops | bytes accessed | tf_op | source)
XLA Modules:
  0.0 1217.0 jit_solution(15423206846366307207)
XLA Ops:
  7.3 76.3 %all-gather.8.cloned.1.call-done = bf16[256,8192]{1,0:T(8,128)(2,1)} async-done(((bf16[256,1024]{1,0:T(8,128)(2,1)}), bf16[256,8192]{1,0:T(8,128)(2,1)}) %all-gather.8.cloned.1.call-update) | async-done | bytes 4194320 | tf_op jit(solution)/shard_map/all_gather | solution.py:25
  83.7 11.5 fusion.5
  95.3 19.8 %psum.14 = f32[256]{0:T(256)S(1)} all-reduce(f32[256]{0:T(256)S(1)} %fusion.6), channel_id=1, replica_groups=mesh['section'=16,'tensor'=8] {'tensor'}, use_global_device_ids=true, to_apply=%region_1.0 | all-reduce | flops 256 | bytes 2048 | tf_op jit(solution)/shard_map/psum | solution.py:31
  116.9 6.2 gather_fusion.2
  123.2 64.0 %all-gather.10.cloned.1.call-done = bf16[256,8192]{1,0:T(8,128)(2,1)} async-done(((bf16[256,1024]{1,0:T(8,128)(2,1)}), bf16[256,8192]{1,0:T(8,128)(2,1)}) %all-gather.10.cloned.1.call-update) | async-done | bytes 4194320 | tf_op jit(solution)/shard_map/all_gather | solution.py:44
  187.2 6.4 copy.20
  193.6 6.2 gather_fusion.3
  201.0 45.5 %gather_fusion = s32[8192]{0:T(1024)S(1)} fusion(s32[8192]{0:T(1024)S(1)} %copy-done, s32[8192]{0:T(1024)S(1)} %broadcast_clamp_fusion.1), kind=kCustom, calls=%fused_computation | custom fusion | bytes 98304 | tf_op jit(solution)/shard_map/jit(_take)/gather | solution.py:45
  246.7 33.7 %gather_fusion.1 = bf16[8192,256]{1,0:T(8,128)(2,1)} fusion(bf16[256,8192]{0,1:T(8,128)(2,1)} %copy.20, s32[8192]{0:T(1024)S(1)} %broadcast_clamp_fusion), kind=kCustom, calls=%fused_computation.1 | custom fusion | bytes 8421376 | tf_op jit(solution)/shard_map/jit(_take)/gather | solution.py:45
  280.4 6.4 copy.21
  286.8 4.5 broadcast_select_fusion
  291.3 4.6 all-to-all-start
  295.9 72.6 %psum.15 = f32[]{:T(128)} all-reduce(f32[]{:T(128)} %get-tuple-element.72), channel_id=1, replica_groups=mesh['section'=16,'tensor'=8] {'section'}, use_global_device_ids=true, to_apply=%region_3.0 | all-reduce | flops 1 | bytes 8 | tf_op jit(solution)/shard_map/psum | solution.py:33
  368.5 8.8 convolution_divide_fusion
  379.4 51.4 %all-gather.14.cloned.1.call-done = f32[512,1024]{0,1:T(8,128)} async-done(((f32[512,128]{0,1:T(8,128)}), f32[512,1024]{0,1:T(8,128)}) %all-gather.14.cloned.1.call-update) | async-done | bytes 2097168 | tf_op jit(solution)/shard_map/all_gather | solution.py:57
  432.8 59.7 %all-gather.16.cloned.1.call-done = f32[2048,1024]{0,1:T(8,128)} async-done(((f32[128,1024]{0,1:T(8,128)}), f32[2048,1024]{0,1:T(8,128)}) %all-gather.16.cloned.1.call-update) | async-done | bytes 8388624 | tf_op jit(solution)/shard_map/all_gather | solution.py:64
  492.6 4.7 slice.274
  497.3 5.5 copy.24
  502.8 4.4 fusion
  509.2 11.7 cholesky.223
  520.9 2.5 cholesky.255
  523.4 9.8 custom-call.62
  533.2 2.4 constant_dynamic-update-slice_fusion.33
  537.2 11.9 cholesky.244
  549.7 9.8 custom-call.63
  562.9 11.7 cholesky.468
  575.2 9.8 custom-call.64
  588.6 12.1 cholesky.487
  601.3 9.8 custom-call.65
  614.6 11.7 cholesky.506
  626.9 10.0 custom-call.66
  640.2 11.7 cholesky.526
  652.5 9.8 custom-call.67
  665.3 11.7 cholesky.546
  677.7 9.8 custom-call.68
  690.1 11.7 cholesky.564
  712.8 4.8 select_select_fusion
  717.6 22.8 %while.1 = (s32[]{:T(128)}, f32[1024,1024]{1,0:T(8,128)}, s32[8,2]{0,1:T(2,128)S(1)}, f32[8,128,128]{2,1,0:T(8,128)S(1)}, s32[]{:T(128)}) while((s32[]{:T(128)}, f32[1024,1024]{1,0:T(8,128)}, s32[8,2]{0,1:T(2,128)S(1)}, f32[8,128,128]{2,1,0:T(8,128)S(1)}, s32[]{:T(128)}) %tuple.63), condition=%wide.while_cond, body=%wide.while_body.sunk | while | flops 2 | bytes 131189 | solution.py:67
  740.5 79.0 %custom-call.69 = f32[8,128,128]{1,2,0:T(8,128)S(1)} custom-call(f32[8,128,128]{2,1,0:T(8,128)S(1)} %get-tuple-element.12), custom_call_target="InvertDiagBlocksLowerTriangular" | custom-call | tf_op jit(solution)/shard_map/triangular_solve | solution.py:67
  836.6 2.5 broadcast_select_fusion.2
  839.1 2.9 copy.34
  842.1 3.1 copy.32
  846.2 166.2 %all-gather.20.cloned.1.call-done = f32[16,512,1024]{2,1,0:T(8,128)} async-done(((f32[1,512,1024]{2,1,0:T(8,128)}), f32[16,512,1024]{2,1,0:T(8,128)}) %all-gather.20.cloned.1.call-update) | async-done | bytes 33554448 | tf_op jit(solution)/shard_map/all_gather | solution.py:13
  1012.3 13.4 %reduce_sum.39 = f32[512,1024]{1,0:T(8,128)} reduce(f32[16,512,1024]{2,1,0:T(8,128)} %all-gather.20.cloned.1.call-done, f32[]{:T(128)} %constant.356.clone.1), dimensions={0}, to_apply=%region_21.22 | reduce | flops 7864320 | bytes 35651588 | tf_op jit(solution)/shard_map/reduce_sum | solution.py:13
  1025.7 159.9 %all-gather.18.cloned.1.call-done = f32[16,512,1024]{2,1,0:T(8,128)} async-done(((f32[1,512,1024]{2,1,0:T(8,128)}), f32[16,512,1024]{2,1,0:T(8,128)}) %all-gather.18.cloned.1.call-update) | async-done | bytes 33554448 | tf_op jit(solution)/shard_map/all_gather | solution.py:13
  1185.7 13.4 %reduce_sum.38 = f32[512,1024]{1,0:T(8,128)} reduce(f32[16,512,1024]{2,1,0:T(8,128)} %all-gather.18.cloned.1.call-done, f32[]{:T(128)} %constant.356.clone.1), dimensions={0}, to_apply=%region_20.21 | reduce | flops 7864320 | bytes 35651588 | tf_op jit(solution)/shard_map/reduce_sum | solution.py:13
  1199.1 2.7 pad_maximum_fusion
  1201.9 6.0 slice_subtract_fusion
  (149 shorter events, 83.6 us)
Async XLA Ops:
  6.5 110.4 %copy-start = (s32[8192]{0:T(1024)S(1)}, s32[8192]{0:T(1024)}, u32[]{:S(2)}) copy-start(s32[8192]{0:T(1024)} %param.7) | copy-start | bytes 98308
  6.5 77.1 %all-gather.8.cloned.1.call-start = ((), (), s32[]{:S(2)}) async-start(), calls=%async_computation.1 | async-start | bytes 4718592 | tf_op jit(solution)/shard_map/all_gather | solution.py:25
  7.3 107.8 %copy-start.7 = (s32[256]{0:T(256)S(1)}, s32[256]{0:T(256)}, u32[]{:S(2)}) copy-start(s32[256]{0:T(256)} %param.6) | copy-start | bytes 3076
  7.3 108.5 %copy-start.6 = (f32[1024]{0:T(1024)S(1)}, f32[1024]{0:T(1024)}, u32[]{:S(2)}) copy-start(f32[1024]{0:T(1024)} %param.11) | copy-start | bytes 12292
  7.3 179.9 %all-gather.10.cloned.1.call-start = ((), (), s32[]{:S(2)}) async-start(), calls=%async_computation.2 | async-start | bytes 4718592 | tf_op jit(solution)/shard_map/all_gather | solution.py:44
  116.7 251.8 %all-gather.12.cloned.1.call-start = ((), (), s32[]{:S(2)}) async-start(), calls=%async_computation.3 | async-start | bytes 8912896 | tf_op jit(solution)/shard_map/all_gather | solution.py:50
  291.3 77.2 %all-to-all-start = ((bf16[256,16,512]{2,0,1:T(8,128)(2,1)}), bf16[256,16,512]{2,0,1:T(8,128)(2,1)}, u32[]{:S(2)}, u32[]{:S(2)}) async-start(bf16[256,16,512]{2,0,1:T(8,128)(2,1)} %broadcast_select_fusion), calls=%async_computation | async-start | bytes 8388608 | tf_op jit(solution)/shard_map/all_to_all | solution.py:46
  295.9 134.9 %all-gather.14.cloned.1.call-start = ((), (), s32[]{:S(2)}) async-start(), calls=%async_computation.4 | async-start | bytes 2359296 | tf_op jit(solution)/shard_map/all_gather | solution.py:57
  377.3 1.3 copy-start.3
  379.3 113.2 %all-gather.16.cloned.1.call-start = ((), (), s32[]{:S(2)}) async-start(), calls=%async_computation.5 | async-start | bytes 8912896 | tf_op jit(solution)/shard_map/all_gather | solution.py:64
  432.7 579.6 %all-gather.20.cloned.1.call-start = ((), (), s32[]{:S(2)}) async-start(), calls=%async_computation.7 | async-start | bytes 35651584 | tf_op jit(solution)/shard_map/all_gather | solution.py:13
  507.2 1.9 copy-start.2
  820.9 2.1 copy-start.5
  842.0 343.6 %all-gather.18.cloned.1.call-start = ((), (), s32[]{:S(2)}) async-start(), calls=%async_computation.6 | async-start | bytes 35651584 | tf_op jit(solution)/shard_map/all_gather | solution.py:13
  1199.1 2.9 copy-start.4
  1207.9 2.0 copy-start.1
Sparse Core Ops, SparseCore 0:
  9.7 73.9 all-gather.7
  116.9 70.3 all-gather.9
  200.9 58.7 all-gather.11
  379.4 51.3 all-gather.13
  432.9 59.6 all-gather.15
  842.1 170.1 all-gather.19
  1014.0 171.6 all-gather.17
